TPU v7x, 32 devices: a whole 2x2x4 slice. The times are simulated.
32 devices in a mesh: sub: 8 (over z, x), grp: 4 (over y, core).
Axes of the slice: x: 2, y: 2, z: 4, core: 2. Of those that a mesh axis runs over, the one named last changes fastest.
Arguments:
- loads: float32 [4, 16, 2, 48, 256], P('grp', 'sub'), may hold values from -18 to 18
- inv_schur: bfloat16 [4, 16, 1024, 1024], P('grp', 'sub'), as said below
- schur: bfloat16 [4, 16, 1024, 1024], P('grp', 'sub'), as said below
- coarse_map: bfloat16 [4, 16, 12, 1024], P('grp', 'sub'), may hold values from -0.75 to 0.75
- coarse_inverse: float32 [4, 16, 12, 4, 192], P('grp', 'sub'), as said below
- face_rows: int32 [4, 16, 1024], P('grp', 'sub'), may hold values from 0 to 1023, each once within a row
- face_len: int32 [4, 16, 2], P('grp', 'sub'), may hold values from 64 to 256
Outputs:
- multipliers: float32 [4, 16, 2, 48, 256], P('grp', 'sub')
- residual: float32 [4, 16, 2, 48, 256], P('grp', 'sub')
Inputs may be any that keep to these rules, and one draw needn't show every extreme that they name: `inv_schur`: each subdomain's matrix is symmetric and positive definite. `schur`: each subdomain's matrix is symmetric and positive definite. `coarse_inverse`: seen as a [768, 768] matrix it is symmetric and positive definite. `face_rows`: each subdomain's row is a permutation of 0 to 1023.
All inputs are finite; a program needn't handle non-finite values.
Results may differ from a plain program's by a relative error of at most 0.025.
Values sent between devices are 32-bit elements; how exact they have to be, the bound alone decides.
A program may use at most 128 MiB of HBM per device.

v0:
```python
import jax
import jax.numpy as jnp
from jax import lax
from jax.sharding import PartitionSpec as P

FACE = 256
LOADS = 48
CDOF = 12
ITERS = 3


def shifted(value, axis, steps):
    count = lax.axis_size(axis)
    initial, last = (max(0, -steps), min(count, count - steps))
    return lax.ppermute(value, axis, [(source, source + steps) for source in range(initial, last)])


def passed_along(block, axis, distance):
    devices = range(lax.axis_size(axis))
    route = [((i - distance) % len(devices), i) for i in devices]
    return lax.ppermute(block, axis, route)


def pair_sum(first, second, pattern):
    return jnp.einsum(pattern, first, second, precision=lax.Precision.HIGHEST)


def combine(weights, faces):
    return jnp.einsum("ab,gksat->gksbt", weights, faces, precision=lax.Precision.HIGHEST)


def gram_solve(matrix, right):
    return jax.scipy.linalg.cho_solve((jnp.linalg.cholesky(matrix), True), right)


def to_slots(faces):
    along = faces[0, :, 0]
    beside_all = faces[0, :, 1]
    from_left = shifted(along[1:2], "sub", 1)
    from_left = jnp.concatenate([from_left, along[0:1]], axis=0)
    from_below = passed_along(beside_all, "grp", 1)
    stacked = jnp.stack([-from_left, along, -from_below, beside_all], axis=2)
    return stacked.reshape(stacked.shape[0], stacked.shape[1], -1)


def to_faces(field, live_mask):
    pieces = field.reshape(field.shape[0], field.shape[1], 4, -1)
    from_right = shifted(pieces[0:1, :, 0], "sub", -1)
    neighbour = jnp.concatenate([pieces[1:2, :, 0], from_right], axis=0)
    from_above = passed_along(pieces[:, :, 2], "grp", -1)
    jumps = jnp.stack([pieces[:, :, 1] - neighbour, pieces[:, :, 3] - from_above], axis=1)
    return jumps[None] * live_mask


def body(loads, inv_schur, schur, coarse_map, coarse_inverse, face_rows, face_len):
    slot_rows = face_rows[0]
    permute = jax.vmap(lambda matrix, ordering: matrix[ordering][:, ordering])
    solve_mats = permute(inv_schur[0], slot_rows)
    dirichlet = permute(schur[0], slot_rows)
    coarse_basis = jax.vmap(lambda basis_rows, ordering: basis_rows[:, ordering])(
        coarse_map[0], slot_rows
    )
    own_rows = coarse_inverse[0].reshape(2 * CDOF, coarse_inverse.shape[3], coarse_inverse.shape[4])
    positions = jnp.arange(FACE)
    column = 2 * lax.axis_index("sub") + jnp.arange(2)
    last_column = 2 * lax.axis_size("sub") - 1
    along_live = (positions[None, :] < face_len[0, :, 0:1]) & (column[:, None] < last_column)
    around_live = positions[None, :] < face_len[0, :, 1:2]
    live_mask = jnp.stack([along_live, around_live], axis=1).astype(jnp.float32)[
        None, :, :, None, :
    ]

    def precondition(resid):
        slotted = to_slots(resid)
        smoothed = jnp.einsum(
            "krm,kmn->krn",
            slotted.astype(jnp.bfloat16),
            dirichlet,
            preferred_element_type=jnp.float32,
        )
        filtered = to_faces(smoothed, live_mask)
        product = lax.psum(pair_sum(filtered, resid, "gksat,gksbt->ab"), ("sub", "grp"))
        return (filtered, product)

    residual = loads * live_mask
    multipliers = jnp.zeros_like(residual)
    search, precond_gram = precondition(residual)
    direction = search
    for iteration in range(ITERS):
        operator_slotted = to_slots(direction)
        rounded = operator_slotted.astype(jnp.bfloat16)
        local_part = jnp.einsum(
            "krm,kmn->krn", rounded, solve_mats, preferred_element_type=jnp.float32
        )
        operator_coarse_terms = jnp.einsum(
            "krm,kqm->krq", rounded, coarse_basis, preferred_element_type=jnp.float32
        )
        flat_terms = jnp.transpose(operator_coarse_terms, (1, 0, 2)).reshape(1, LOADS, 2 * CDOF)
        cycle_terms = lax.all_gather(flat_terms, "grp", axis=0, tiled=True)
        solved = jnp.einsum(
            "grx,kgx->rk",
            lax.all_gather(cycle_terms, "sub", axis=2, tiled=True),
            own_rows,
            precision=lax.Precision.HIGHEST,
        )
        corrections = jnp.transpose(solved.reshape(LOADS, 2, CDOF), (1, 0, 2)).astype(jnp.bfloat16)
        response = local_part + jnp.einsum(
            "krq,kqm->krm", corrections, coarse_basis, preferred_element_type=jnp.float32
        )
        image_faces = to_faces(response, live_mask)
        curvature = lax.psum(pair_sum(direction, image_faces, "gksat,gksbt->ab"), ("sub", "grp"))
        image_faces, curvature = (image_faces, curvature)
        step_size = gram_solve(curvature, precond_gram)
        multipliers = multipliers + combine(step_size, direction)
        residual = residual - combine(step_size, image_faces)
        if iteration + 1 < ITERS:
            search, new_gram = precondition(residual)
            conjugate = gram_solve(precond_gram, new_gram)
            direction = search + combine(conjugate, direction)
            precond_gram = new_gram
    return (multipliers, residual)


def solution(mesh):
    in_specs = (
        P("grp", "sub", None, None, None),
        P("grp", "sub", None, None),
        P("grp", "sub", None, None),
        P("grp", "sub", None, None),
        P("grp", "sub", None, None, None),
        P("grp", "sub", None),
        P("grp", "sub", None),
    )
    out_specs = (P("grp", "sub", None, None, None), P("grp", "sub", None, None, None))
    return jax.shard_map(body, mesh=mesh, in_specs=in_specs, out_specs=out_specs, check_vma=False)
```

profile of v0, /device:TPU:10, one launch (start us, length us, event | category | flops | bytes accessed | tf_op | source)
XLA Modules:
  0.0 658.3 jit_solution(1124318638356162383)
XLA Ops:
  7.0 41.9 %gather_fusion = bf16[2048,1024]{1,0:T(8,128)(2,1)} fusion(bf16[2,1024,1024]{2,1,0:T(8,128)(2,1)} %bitcast.533, s32[2048]{0:T(1024)S(1)} %bitcast.528), kind=kCustom, calls=%fused_computation | custom fusion | bytes 8404992 | tf_op jit(solution)/shard_map/vmap()/gather | solution.py:57
  48.9 6.2 copy.171
  55.2 40.3 %gather_fusion.1 = bf16[2048,1024]{1,0:T(8,128)(2,1)} fusion(bf16[2,1024,1024]{1,2,0:T(8,128)(2,1)} %copy.171, s32[2048]{0:T(1024)S(1)} %bitcast.529), kind=kCustom, calls=%fused_computation.1 | custom fusion | bytes 8404992 | tf_op jit(solution)/shard_map/vmap()/gather | solution.py:57
  95.5 42.0 %gather_fusion.2 = bf16[2048,1024]{1,0:T(8,128)(2,1)} fusion(bf16[2,1024,1024]{2,1,0:T(8,128)(2,1)} %bitcast.534, s32[2048]{0:T(1024)S(1)} %bitcast.530), kind=kCustom, calls=%fused_computation.2 | custom fusion | bytes 8404992 | tf_op jit(solution)/shard_map/vmap()/gather | solution.py:57
  137.5 6.2 copy.182
  143.8 40.4 %gather_fusion.3 = bf16[2048,1024]{1,0:T(8,128)(2,1)} fusion(bf16[2,1024,1024]{1,2,0:T(8,128)(2,1)} %copy.182, s32[2048]{0:T(1024)S(1)} %bitcast.531), kind=kCustom, calls=%fused_computation.3 | custom fusion | bytes 8404992 | tf_op jit(solution)/shard_map/vmap()/gather | solution.py:57
  184.5 11.1 %gather_fusion.4 = bf16[2048,12]{1,0:T(8,128)(2,1)S(1)} fusion(bf16[2,12,1024]{1,2,0:T(8,128)(2,1)S(1)} %bitcast.549, s32[2048]{0:T(1024)S(1)} %bitcast.532), kind=kCustom, calls=%fused_computation.4 | custom fusion | bytes 114688 | tf_op jit(solution)/shard_map/vmap()/gather | solution.py:60
  216.7 5.2 all_gather.18
  221.9 26.2 %all_gather.19 = f32[4,48,192]{1,2,0:T(8,128)S(1)} all-gather(f32[4,48,24]{1,2,0:T(8,128)S(1)} %all_gather.18), channel_id=1, replica_groups=mesh['sub'=8,'grp'=4] {'sub'}, dimensions={2}, use_global_device_ids=true | all-gather | bytes 165888 | tf_op jit(solution)/shard_map/all_gather | solution.py:102
  256.8 43.6 %all-reduce = (f32[48,48]{0,1:T(8,128)S(1)}, f32[48,48]{0,1:T(8,128)S(1)}) all-reduce(f32[48,48]{0,1:T(8,128)S(1)} %convolution_bitcast_fusion.14, f32[48,48]{0,1:T(8,128)S(1)} %convolution_bitcast_fusion.15), channel_id=1, replica_groups=mesh['sub'=8,'grp'=4] {'sub','grp'}, use_global_device_ids=true, to_apply=%region_3.5 | all-reduce | flops 4608 | bytes 36864 | tf_op jit(solution)/shard_map/psum | solution.py:82
  300.6 4.4 cholesky.89
  313.2 4.4 cholesky.100
  334.8 40.7 %psum.44 = f32[48,48]{0,1:T(8,128)S(1)} all-reduce(f32[48,48]{0,1:T(8,128)S(1)} %convolution_bitcast_fusion.13), channel_id=1, replica_groups=mesh['sub'=8,'grp'=4] {'sub','grp'}, use_global_device_ids=true, to_apply=%region_4.0 | all-reduce | flops 2304 | bytes 18432 | tf_op jit(solution)/shard_map/psum | solution.py:82
  395.8 5.4 all_gather.20
  401.2 26.6 %all_gather.21 = f32[4,48,192]{1,2,0:T(8,128)S(1)} all-gather(f32[4,48,24]{1,2,0:T(8,128)S(1)} %all_gather.20), channel_id=1, replica_groups=mesh['sub'=8,'grp'=4] {'sub'}, dimensions={2}, use_global_device_ids=true | all-gather | bytes 165888 | tf_op jit(solution)/shard_map/all_gather | solution.py:102
  428.7 5.9 collective-permute-start.14
  437.8 43.5 %psum.45 = f32[48,48]{0,1:T(8,128)S(1)} all-reduce(f32[48,48]{0,1:T(8,128)S(1)} %convolution_bitcast_fusion.12), channel_id=1, replica_groups=mesh['sub'=8,'grp'=4] {'sub','grp'}, use_global_device_ids=true, to_apply=%region_5.0 | all-reduce | flops 2304 | bytes 18432 | tf_op jit(solution)/shard_map/psum | solution.py:111
  481.4 4.4 cholesky.111
  508.8 41.7 %psum.46 = f32[48,48]{1,0:T(8,128)S(1)} all-reduce(f32[48,48]{1,0:T(8,128)S(1)} %convolution_bitcast_fusion.11), channel_id=1, replica_groups=mesh['sub'=8,'grp'=4] {'sub','grp'}, use_global_device_ids=true, to_apply=%region_6.9 | all-reduce | flops 2304 | bytes 18432 | tf_op jit(solution)/shard_map/psum | solution.py:82
  561.3 5.4 all_gather.22
  566.7 26.5 %all_gather.23 = f32[4,48,192]{1,2,0:T(8,128)S(1)} all-gather(f32[4,48,24]{1,2,0:T(8,128)S(1)} %all_gather.22), channel_id=1, replica_groups=mesh['sub'=8,'grp'=4] {'sub'}, dimensions={2}, use_global_device_ids=true | all-gather | bytes 165888 | tf_op jit(solution)/shard_map/all_gather | solution.py:102
  594.2 5.9 collective-permute-start.22
  603.0 43.4 %psum.47 = f32[48,48]{0,1:T(8,128)S(1)} all-reduce(f32[48,48]{0,1:T(8,128)S(1)} %convolution_bitcast_fusion.10), channel_id=1, replica_groups=mesh['sub'=8,'grp'=4] {'sub','grp'}, use_global_device_ids=true, to_apply=%region_7.10 | all-reduce | flops 2304 | bytes 18432 | tf_op jit(solution)/shard_map/psum | solution.py:111
  646.4 4.4 cholesky.133
  (233 shorter events, 130.4 us)
Async XLA Ops:
  2.7 193.0 %collective-permute-start = (f32[1,48,256]{2,1,0:T(8,128)S(1)}, f32[1,48,256]{2,1,0:T(8,128)S(1)}, u32[]{:S(2)}, u32[]{:S(2)}) collective-permute-start(f32[1,48,256]{2,1,0:T(8,128)S(1)} %get-tuple-element.64), channel_id=1, source_target_pairs={{0,4},{4,8},{8,12},{12,16},{16,20},{20,24},{24,28},{1,5},{5,9},{9,... | collective-permute-start | bytes 147464 | tf_op jit(solution)/shard_map/ppermute | solution.py:15
  6.2 189.5 %collective-permute-start.1 = (f32[2,48,256]{2,1,0:T(8,128)S(1)}, f32[2,48,256]{2,1,0:T(8,128)S(1)}, u32[]{:S(2)}, u32[]{:S(2)}) collective-permute-start(f32[2,48,256]{2,1,0:T(8,128)S(1)} %slice_bitcast_fusion.5), channel_id=1, source_target_pairs={{3,0},{0,1},{1,2},{2,3},{7,4},{4,5},{5,6},{6,7},{11,8},{8,9},{9,10... | collective-permute-start | bytes 294920 | tf_op jit(solution)/shard_map/ppermute | solution.py:21
  199.6 7.1 %collective-permute-start.2 = (f32[1,48,256]{2,1,0:T(8,128)S(1)}, f32[1,48,256]{2,1,0:T(8,128)S(1)}, u32[]{:S(2)}, u32[]{:S(2)}) collective-permute-start(f32[1,48,256]{2,1,0:T(8,128)S(1)} %bitcast.587), channel_id=1, source_target_pairs={{4,0},{8,4},{12,8},{16,12},{20,16},{24,20},{28,24},{5,1},{9,5},{13... | collective-permute-start | bytes 147464 | tf_op jit(solution)/shard_map/ppermute | solution.py:15
  202.6 4.2 collective-permute-start.3
  206.9 6.2 collective-permute-start.4
  210.9 4.1 collective-permute-start.5
  249.1 6.9 %collective-permute-start.6 = (f32[1,48,256]{2,1,0:T(8,128)S(1)}, f32[1,48,256]{2,1,0:T(8,128)S(1)}, u32[]{:S(2)}, u32[]{:S(2)}) collective-permute-start(f32[1,48,256]{2,1,0:T(8,128)S(1)} %bitcast.588), channel_id=1, source_target_pairs={{4,0},{8,4},{12,8},{16,12},{20,16},{24,20},{28,24},{5,1},{9,5},{13... | collective-permute-start | bytes 147464 | tf_op jit(solution)/shard_map/ppermute | solution.py:15
  253.7 2.5 collective-permute-start.7
  311.2 11.4 %collective-permute-start.8 = (f32[1,48,256]{2,1,0:T(8,128)S(1)}, f32[1,48,256]{2,1,0:T(8,128)S(1)}, u32[]{:S(2)}, u32[]{:S(2)}) collective-permute-start(f32[1,48,256]{2,1,0:T(8,128)S(1)} %get-tuple-element.54), channel_id=1, source_target_pairs={{0,4},{4,8},{8,12},{12,16},{16,20},{20,24},{24,28},{1,5},{5,9},{9,... | collective-permute-start | bytes 147464 | tf_op jit(solution)/shard_map/ppermute | solution.py:15
  313.1 9.5 %collective-permute-start.9 = (f32[2,48,256]{2,1,0:T(8,128)S(1)}, f32[2,48,256]{2,1,0:T(8,128)S(1)}, u32[]{:S(2)}, u32[]{:S(2)}) collective-permute-start(f32[2,48,256]{2,1,0:T(8,128)S(1)} %slice_bitcast_fusion.3), channel_id=1, source_target_pairs={{3,0},{0,1},{1,2},{2,3},{7,4},{4,5},{5,6},{6,7},{11,8},{8,9},{9,10... | collective-permute-start | bytes 294920 | tf_op jit(solution)/shard_map/ppermute | solution.py:21
  326.6 6.9 %collective-permute-start.10 = (f32[1,48,256]{2,1,0:T(8,128)S(1)}, f32[1,48,256]{2,1,0:T(8,128)S(1)}, u32[]{:S(2)}, u32[]{:S(2)}) collective-permute-start(f32[1,48,256]{2,1,0:T(8,128)S(1)} %bitcast.589), channel_id=1, source_target_pairs={{4,0},{8,4},{12,8},{16,12},{20,16},{24,20},{28,24},{5,1},{9,5},{13... | collective-permute-start | bytes 147464 | tf_op jit(solution)/shard_map/ppermute | solution.py:15
  330.8 3.7 collective-permute-start.11
  381.6 6.3 collective-permute-start.12
  387.8 4.1 collective-permute-start.13
  428.7 7.7 %collective-permute-start.14 = (f32[1,48,256]{2,1,0:T(8,128)S(1)}, f32[1,48,256]{2,1,0:T(8,128)S(1)}, u32[]{:S(2)}, u32[]{:S(2)}) collective-permute-start(f32[1,48,256]{2,1,0:T(8,128)S(1)} %bitcast.590), channel_id=1, source_target_pairs={{4,0},{8,4},{12,8},{16,12},{20,16},{24,20},{28,24},{5,1},{9,5},{13... | collective-permute-start | bytes 147464 | tf_op jit(solution)/shard_map/ppermute | solution.py:15
  434.9 2.5 collective-permute-start.15
  491.6 6.0 collective-permute-start.16
  493.5 4.1 collective-permute-start.17
  501.5 6.9 %collective-permute-start.18 = (f32[1,48,256]{2,1,0:T(8,128)S(1)}, f32[1,48,256]{2,1,0:T(8,128)S(1)}, u32[]{:S(2)}, u32[]{:S(2)}) collective-permute-start(f32[1,48,256]{2,1,0:T(8,128)S(1)} %bitcast.591), channel_id=1, source_target_pairs={{4,0},{8,4},{12,8},{16,12},{20,16},{24,20},{28,24},{5,1},{9,5},{13... | collective-permute-start | bytes 147464 | tf_op jit(solution)/shard_map/ppermute | solution.py:15
  505.8 2.7 collective-permute-start.19
  551.3 6.0 collective-permute-start.20
  553.3 4.1 collective-permute-start.21
  594.2 7.6 %collective-permute-start.22 = (f32[1,48,256]{2,1,0:T(8,128)S(1)}, f32[1,48,256]{2,1,0:T(8,128)S(1)}, u32[]{:S(2)}, u32[]{:S(2)}) collective-permute-start(f32[1,48,256]{2,1,0:T(8,128)S(1)} %bitcast.592), channel_id=1, source_target_pairs={{4,0},{8,4},{12,8},{16,12},{20,16},{24,20},{28,24},{5,1},{9,5},{13... | collective-permute-start | bytes 147464 | tf_op jit(solution)/shard_map/ppermute | solution.py:15
  600.4 2.3 collective-permute-start.23
  (3 other events, 303.4 us)
where the time goes:
time: 662 us; the launch traced here: 658 us
  blocking collectives  308 us (47%)
  local copies, waits for them, and re-layouts  193 us (29%)
  other arithmetic  49.2 us (7%)
  starting transfers between devices  47 us (7%)
  matrix products  30.1 us (5%)
  waiting for transfers between devices  28.4 us (4%)
    gather x6, local copies, waits for them, and re-layouts, body(): permute = jax.vmap(lambda matrix, ordering: matrix[ordering][:, ordering])  177 us
    psum x3, blocking collectives, precondition(): lax.psum(pair_sum(filtered, resid, 'gksat,gksbt->ab'), ('sub', 'grp'))  126 us
    psum x2, blocking collectives, body(): lax.psum(pair_sum(direction, image_faces, 'gksat,gksbt->ab'), ('sub', 'gr...  86.9 us
    all_gather x3, blocking collectives, body(): lax.all_gather(cycle_terms, 'sub', axis=2, tiled=True)  79.3 us
    ppermute x12, starting transfers between devices, shifted(): lax.ppermute(value, axis, [(source, source + steps) for source in range(i...  41.7 us
    another operation x15, other arithmetic, gram_solve(): jnp.linalg.cholesky(matrix)  25.3 us
    another operation x10, other arithmetic, gram_solve(): jax.scipy.linalg.cho_solve((jnp.linalg.cholesky(matrix), True), right)  21.6 us
    ppermute x12, waiting for transfers between devices, shifted(): lax.ppermute(value, axis, [(source, source + steps) for source in range(i...  19.5 us
  transfers between devices with their start and end apart: 24, of which 15 were waited for; matrix products, arithmetic and copies ran while one was open for 31% of the time, Pallas kernels for 0%

commit v1 on v0

--- a/solution.py
+++ b/solution.py
@@ -108,7 +108,10 @@
             "krq,kqm->krm", corrections, coarse_basis, preferred_element_type=jnp.float32
         )
         image_faces = to_faces(response, live_mask)
-        curvature = lax.psum(pair_sum(direction, image_faces, "gksat,gksbt->ab"), ("sub", "grp"))
+        curvature = jnp.sum(
+            lax.all_gather(pair_sum(direction, image_faces, "gksat,gksbt->ab"), ("sub", "grp")),
+            axis=0,
+        )
         image_faces, curvature = (image_faces, curvature)
         step_size = gram_solve(curvature, precond_gram)
         multipliers = multipliers + combine(step_size, direction)

time: 662 us -> 699 us (1.056)
  the two profiles are of different devices: /device:TPU:10 before, /device:TPU:0 now
where the time goes in v1:
time: 699 us; the launch traced here: 696 us
  blocking collectives  347 us (50%)
  local copies, waits for them, and re-layouts  194 us (28%)
  other arithmetic  49.5 us (7%)
  waiting for transfers between devices  37.1 us (5%)
  starting transfers between devices  36.3 us (5%)
  matrix products  30.1 us (4%)
    gather x6, local copies, waits for them, and re-layouts, body(): permute = jax.vmap(lambda matrix, ordering: matrix[ordering][:, ordering])  178 us
    all_gather x3, blocking collectives, body(): lax.all_gather(pair_sum(direction, image_faces, 'gksat,gksbt->ab'), ('sub...  121 us
    psum x3, blocking collectives, precondition(): lax.psum(pair_sum(filtered, resid, 'gksat,gksbt->ab'), ('sub', 'grp'))  117 us
    all_gather x3, blocking collectives, body(): lax.all_gather(cycle_terms, 'sub', axis=2, tiled=True)  93.4 us
    ppermute x12, starting transfers between devices, shifted(): lax.ppermute(value, axis, [(source, source + steps) for source in range(i...  30.9 us
    ppermute x12, waiting for transfers between devices, shifted(): lax.ppermute(value, axis, [(source, source + steps) for source in range(i...  26.1 us
    another operation x15, other arithmetic, gram_solve(): jnp.linalg.cholesky(matrix)  25.3 us
    another operation x10, other arithmetic, gram_solve(): jax.scipy.linalg.cho_solve((jnp.linalg.cholesky(matrix), True), right)  21.6 us
  transfers between devices with their start and end apart: 24, of which 13 were waited for; matrix products, arithmetic and copies ran while one was open for 30% of the time, Pallas kernels for 0%

profile of v1, /device:TPU:0, one launch (start us, length us, event | category | flops | bytes accessed | tf_op | source)
XLA Modules:
  0.0 695.8 jit_solution(12960999615292255584)
XLA Ops:
  2.7 4.8 collective-permute-start
  8.4 42.0 %gather_fusion = bf16[2048,1024]{1,0:T(8,128)(2,1)} fusion(bf16[2,1024,1024]{2,1,0:T(8,128)(2,1)} %bitcast.542, s32[2048]{0:T(1024)S(1)} %bitcast.537), kind=kCustom, calls=%fused_computation | custom fusion | bytes 8404992 | tf_op jit(solution)/shard_map/vmap()/gather | solution.py:57
  50.4 6.2 copy.165
  56.6 40.5 %gather_fusion.1 = bf16[2048,1024]{1,0:T(8,128)(2,1)} fusion(bf16[2,1024,1024]{1,2,0:T(8,128)(2,1)} %copy.165, s32[2048]{0:T(1024)S(1)} %bitcast.538), kind=kCustom, calls=%fused_computation.1 | custom fusion | bytes 8404992 | tf_op jit(solution)/shard_map/vmap()/gather | solution.py:57
  97.2 42.0 %gather_fusion.2 = bf16[2048,1024]{1,0:T(8,128)(2,1)} fusion(bf16[2,1024,1024]{2,1,0:T(8,128)(2,1)} %bitcast.543, s32[2048]{0:T(1024)S(1)} %bitcast.539), kind=kCustom, calls=%fused_computation.2 | custom fusion | bytes 8404992 | tf_op jit(solution)/shard_map/vmap()/gather | solution.py:57
  139.2 6.2 copy.176
  145.4 40.6 %gather_fusion.3 = bf16[2048,1024]{1,0:T(8,128)(2,1)} fusion(bf16[2,1024,1024]{1,2,0:T(8,128)(2,1)} %copy.176, s32[2048]{0:T(1024)S(1)} %bitcast.540), kind=kCustom, calls=%fused_computation.3 | custom fusion | bytes 8404992 | tf_op jit(solution)/shard_map/vmap()/gather | solution.py:57
  186.3 11.1 %gather_fusion.4 = bf16[2048,12]{1,0:T(8,128)(2,1)S(1)} fusion(bf16[2,12,1024]{1,2,0:T(8,128)(2,1)S(1)} %bitcast.561, s32[2048]{0:T(1024)S(1)} %bitcast.541), kind=kCustom, calls=%fused_computation.4 | custom fusion | bytes 114688 | tf_op jit(solution)/shard_map/vmap()/gather | solution.py:60
  217.8 5.2 all_gather.36
  223.0 31.3 %all_gather.37 = f32[4,48,192]{1,2,0:T(8,128)S(1)} all-gather(f32[4,48,24]{1,2,0:T(8,128)S(1)} %all_gather.36), channel_id=1, replica_groups=mesh['sub'=8,'grp'=4] {'sub'}, dimensions={2}, use_global_device_ids=true | all-gather | bytes 165888 | tf_op jit(solution)/shard_map/all_gather | solution.py:102
  262.0 40.3 %all-gather = f32[1536,48]{1,0:T(8,128)S(1)} all-gather(f32[48,48]{1,0:T(8,128)S(1)} %convolution_bitcast_fusion.15), channel_id=2, replica_groups=mesh['sub'=8,'grp'=4] {'sub','grp'}, dimensions={0}, use_global_device_ids=true | all-gather | bytes 304128 | tf_op jit(solution)/shard_map/all_gather | solution.py:112
  302.5 4.4 cholesky.89
  311.9 37.1 %psum.21 = f32[48,48]{0,1:T(8,128)S(1)} all-reduce(f32[48,48]{0,1:T(8,128)S(1)} %convolution_bitcast_fusion.14), channel_id=1, replica_groups=mesh['sub'=8,'grp'=4] {'sub','grp'}, use_global_device_ids=true, to_apply=%region_3.5 | all-reduce | flops 2304 | bytes 18432 | tf_op jit(solution)/shard_map/psum | solution.py:82
  374.2 41.8 %psum.22 = f32[48,48]{0,1:T(8,128)S(1)} all-reduce(f32[48,48]{0,1:T(8,128)S(1)} %convolution_bitcast_fusion.13), channel_id=1, replica_groups=mesh['sub'=8,'grp'=4] {'sub','grp'}, use_global_device_ids=true, to_apply=%region_4.0 | all-reduce | flops 2304 | bytes 18432 | tf_op jit(solution)/shard_map/psum | solution.py:82
  417.0 4.4 cholesky.122
  438.6 5.2 all_gather.40
  443.8 31.2 %all_gather.41 = f32[4,48,192]{1,2,0:T(8,128)S(1)} all-gather(f32[4,48,24]{1,2,0:T(8,128)S(1)} %all_gather.40), channel_id=1, replica_groups=mesh['sub'=8,'grp'=4] {'sub'}, dimensions={2}, use_global_device_ids=true | all-gather | bytes 165888 | tf_op jit(solution)/shard_map/all_gather | solution.py:102
  482.3 40.6 %all-gather.1 = f32[1536,48]{1,0:T(8,128)S(1)} all-gather(f32[48,48]{1,0:T(8,128)S(1)} %convolution_bitcast_fusion.12), channel_id=3, replica_groups=mesh['sub'=8,'grp'=4] {'sub','grp'}, dimensions={0}, use_global_device_ids=true | all-gather | bytes 304128 | tf_op jit(solution)/shard_map/all_gather | solution.py:112
  523.1 4.4 cholesky.111
  549.0 38.2 %psum.23 = f32[48,48]{1,0:T(8,128)S(1)} all-reduce(f32[48,48]{1,0:T(8,128)S(1)} %convolution_bitcast_fusion.11), channel_id=1, replica_groups=mesh['sub'=8,'grp'=4] {'sub','grp'}, use_global_device_ids=true, to_apply=%region_6.9 | all-reduce | flops 2304 | bytes 18432 | tf_op jit(solution)/shard_map/psum | solution.py:82
  600.3 5.2 all_gather.44
  605.5 31.0 %all_gather.45 = f32[4,48,192]{1,2,0:T(8,128)S(1)} all-gather(f32[4,48,24]{1,2,0:T(8,128)S(1)} %all_gather.44), channel_id=1, replica_groups=mesh['sub'=8,'grp'=4] {'sub'}, dimensions={2}, use_global_device_ids=true | all-gather | bytes 165888 | tf_op jit(solution)/shard_map/all_gather | solution.py:102
  643.8 39.9 %all-gather.2 = f32[1536,48]{1,0:T(8,128)S(1)} all-gather(f32[48,48]{1,0:T(8,128)S(1)} %convolution_bitcast_fusion.10), channel_id=4, replica_groups=mesh['sub'=8,'grp'=4] {'sub','grp'}, dimensions={0}, use_global_device_ids=true | all-gather | bytes 304128 | tf_op jit(solution)/shard_map/all_gather | solution.py:112
  683.9 4.4 cholesky.133
  (237 shorter events, 135.5 us)
Async XLA Ops:
  2.7 194.8 %collective-permute-start = (f32[1,48,256]{2,1,0:T(8,128)S(1)}, f32[1,48,256]{2,1,0:T(8,128)S(1)}, u32[]{:S(2)}, u32[]{:S(2)}) collective-permute-start(f32[1,48,256]{2,1,0:T(8,128)S(1)} %get-tuple-element.62), channel_id=1, source_target_pairs={{0,4},{4,8},{8,12},{12,16},{16,20},{20,24},{24,28},{1,5},{5,9},{9,... | collective-permute-start | bytes 147464 | tf_op jit(solution)/shard_map/ppermute | solution.py:15
  7.6 189.9 %collective-permute-start.1 = (f32[2,48,256]{2,1,0:T(8,128)S(1)}, f32[2,48,256]{2,1,0:T(8,128)S(1)}, u32[]{:S(2)}, u32[]{:S(2)}) collective-permute-start(f32[2,48,256]{2,1,0:T(8,128)S(1)} %slice_bitcast_fusion.5), channel_id=1, source_target_pairs={{3,0},{0,1},{1,2},{2,3},{7,4},{4,5},{5,6},{6,7},{11,8},{8,9},{9,10... | collective-permute-start | bytes 294920 | tf_op jit(solution)/shard_map/ppermute | solution.py:21
  201.4 6.4 collective-permute-start.2
  203.3 4.6 collective-permute-start.3
  207.9 5.9 collective-permute-start.4
  212.0 4.1 collective-permute-start.5
  255.3 6.0 collective-permute-start.6
  256.9 4.4 collective-permute-start.7
  350.2 13.7 %collective-permute-start.8 = (f32[1,48,256]{2,1,0:T(8,128)S(1)}, f32[1,48,256]{2,1,0:T(8,128)S(1)}, u32[]{:S(2)}, u32[]{:S(2)}) collective-permute-start(f32[1,48,256]{2,1,0:T(8,128)S(1)} %get-tuple-element.52), channel_id=1, source_target_pairs={{0,4},{4,8},{8,12},{12,16},{16,20},{20,24},{24,28},{1,5},{5,9},{9,... | collective-permute-start | bytes 147464 | tf_op jit(solution)/shard_map/ppermute | solution.py:15
  354.4 9.5 %collective-permute-start.9 = (f32[2,48,256]{2,1,0:T(8,128)S(1)}, f32[2,48,256]{2,1,0:T(8,128)S(1)}, u32[]{:S(2)}, u32[]{:S(2)}) collective-permute-start(f32[2,48,256]{2,1,0:T(8,128)S(1)} %slice_bitcast_fusion.3), channel_id=1, source_target_pairs={{3,0},{0,1},{1,2},{2,3},{7,4},{4,5},{5,6},{6,7},{11,8},{8,9},{9,10... | collective-permute-start | bytes 294920 | tf_op jit(solution)/shard_map/ppermute | solution.py:21
  367.8 6.0 collective-permute-start.10
  369.4 4.5 collective-permute-start.11
  422.1 8.5 %collective-permute-start.12 = (f32[1,48,256]{2,1,0:T(8,128)S(1)}, f32[1,48,256]{2,1,0:T(8,128)S(1)}, u32[]{:S(2)}, u32[]{:S(2)}) collective-permute-start(f32[1,48,256]{2,1,0:T(8,128)S(1)} %get-tuple-element.46), channel_id=1, source_target_pairs={{0,4},{4,8},{8,12},{12,16},{16,20},{20,24},{24,28},{1,5},{5,9},{9,... | collective-permute-start | bytes 147464 | tf_op jit(solution)/shard_map/ppermute | solution.py:15
  430.6 4.1 collective-permute-start.13
  476.0 6.0 collective-permute-start.14
  477.8 4.2 collective-permute-start.15
  533.3 3.1 collective-permute-start.16
  534.6 4.1 collective-permute-start.17
  542.7 6.0 collective-permute-start.18
  544.2 4.4 collective-permute-start.19
  588.0 5.9 collective-permute-start.20
  592.2 4.1 collective-permute-start.21
  637.5 6.0 collective-permute-start.22
  639.0 4.4 collective-permute-start.23
  (3 other events, 309.1 us)
